TPU v7x, 512 devices: a whole 4x8x8 slice. The times are simulated.
512 devices in a mesh: lat: 16 (over z_lo, y), lon: 32 (over x, z_hi, core).
Axes of the slice: x: 4, y: 8, z: 8 (z_hi: 4, z_lo: 2; z = z_hi * 2 + z_lo), core: 2. Of those that a mesh axis runs over, the one named last changes fastest.
Arguments:
- fine_in: bfloat16 [4, 192, 384, 512], P(None, 'lat', 'lon'), may hold values from -6 to 6
- norm_gain: float32 [512], replicated, may hold values from 0.5 to 1.5
- qkv_weight: bfloat16 [512, 1536], replicated, as said below
- proj_weight: bfloat16 [512, 512], replicated, may hold values from -0.25 to 0.25
- merge_gain: float32 [2048], replicated, may hold values from 0.5 to 1.5
- merge_weight: bfloat16 [2048, 1024], P('lon'), may hold values from -0.125 to 0.125
Outputs:
- fine_out: bfloat16 [4, 192, 384, 512], P(None, 'lat', 'lon')
- coarse: bfloat16 [4, 96, 192, 1024], P(None, 'lat', 'lon')
Inputs may be any that keep to these rules, and one draw needn't show every extreme that they name: `qkv_weight`: query, key and value projections.
All inputs are finite; a program needn't handle non-finite values.
Results may differ from a plain program's by a relative error of at most 0.0067.
Values may be sent and summed in bfloat16 or wider, within the bound.
A program may use at most 128 MiB of HBM per device.

v0:
```python
import functools

import jax
import jax.numpy as jnp
import numpy as np
from jax import lax
from jax.experimental import pallas as pl
from jax.experimental.pallas import tpu as pltpu
from jax.sharding import PartitionSpec as P

MESH = pl.DeviceIdType.MESH
BF16 = jnp.bfloat16
F32 = jnp.float32

WIDTH = 512
PAIRS = 4
WIN = 144
LEVELS = ((1, 2), (3, 0))
TILE = 576
SENT = ((0, 80), (80, 48), (128, 48), (176, 48))
OWN = 224
PIECES = 352


def tables():
    forward = np.zeros((2, PIECES, TILE), np.float32)
    quad = np.zeros((2, 288, TILE), np.float32)
    order = np.zeros((144, 144), np.float32)
    for pair in range(2):
        lo, hi = range(0, 6), range(6, 12)
        sent_rows, kept_rows = (lo, hi) if pair == 0 else (hi, lo)
        first, mid, last = range(0, 3), range(3, 9), range(9, 12)
        sent_cols, kept_cols = (first, last) if pair == 0 else (last, first)

        def put(at, rows, cols):
            for level in LEVELS[pair]:
                for r in rows:
                    for c in cols:
                        forward[pair, at, (r * 12 + c) * 4 + level] = 1
                        at += 1

        put(0, sent_rows, mid)
        put(80 + 8, sent_rows, kept_cols)
        put(128 + 4, kept_rows, sent_cols)
        put(176 + 12, sent_rows, sent_cols)
        put(OWN + 8, kept_rows, mid)
        put(OWN + 80, kept_rows, kept_cols)
        for l, level in enumerate(LEVELS[pair]):
            for r in range(12):
                for c in range(12):
                    q, at = (r % 2) + 2 * (c % 2), (r // 2) * 6 + c // 2
                    quad[pair, q * 72 + l * 36 + at, (r * 12 + c) * 4 + level] = 1
                    order[at * 4 + level, pair * 72 + l * 36 + at] = 1
    back = np.concatenate([forward[0].T, forward[1].T], 1)
    backq = np.stack([quad[pair] @ forward[pair].T for pair in range(2)])
    return [table.astype(BF16) for table in (forward, back, backq, quad, order)]


def dot(a, b):
    return jnp.dot(a, b, preferred_element_type=F32)


def kernel(
    fine_ref, ngain_ref, qkvw_ref, projw_ref, mgain_ref, shard_ref, fwd_ref, back_ref, backq_ref, quad_ref, order_ref,
    out_ref, coarse_ref,
    xin, xraw, xn, fwd, rx, xw, att, bsend, back, xquad, mask, mn, merged, out, wbuf,
    qkvw, projw, fwd_t, back_t, backq_t, quad_t, order_t, send, recv, local,
):
    ny = lax.axis_size("lat") // 2
    nlat, nlon = lax.axis_size("lat"), lax.axis_size("lon")
    lat, lon = lax.axis_index("lat"), lax.axis_index("lon")
    y, m = lat % ny, lat // ny
    gx, gk, core = lon // 8, (lon // 2) % 4, lon % 2
    up, down = (lat + nlat - 1) % nlat, (lat + 1) % nlat
    left, right = (lon + nlon - 1) % nlon, (lon + 1) % nlon

    xm, xp, xo = (gx + 3) % 4, (gx + 1) % 4, (gx + 2) % 4
    ko = (gk + 3 + 2 * m) % 4
    ki = (gk + 1 + 2 * m) % 4
    kf = (gk + 2) % 4
    olat = (1 - m) * ny + y
    dev_xp = (lat, xp * 8 + gk * 2 + core)
    dev_xm = (lat, xm * 8 + gk * 2 + core)
    dev_o = (olat, gx * 8 + ko * 2 + core)
    dev_i = (olat, lon)
    dev_far = (olat, gx * 8 + kf * 2 + core)
    dev_s = (lat, lon + 1 - 2 * core)
    to = (((up, lon), (up, lon), (lat, left), (up, left)), ((down, lon), (down, lon), (lat, right), (down, right)))
    frm = (to[1], to[0])

    barrier = pltpu.get_barrier_semaphore()
    partners = [*to[0][1:], *to[1][1:], dev_xp, dev_xm, dev_o, dev_i, dev_far, dev_s]
    for device in partners:
        pl.semaphore_signal(barrier, inc=1, device_id=device, device_id_type=MESH)

    copies = []

    def load(src, dst):
        copy = pltpu.make_async_copy(src, dst, local.at[len(copies)])
        copy.start()
        copies.append(copy)
        return copy

    load_x = load(fine_ref, xin)
    load_f = load(fwd_ref, fwd_t)
    load_qkv = load(qkvw_ref, qkvw)
    load_q = load(quad_ref, quad_t)
    load_proj = load(projw_ref, projw)
    load_bq = load(backq_ref, backq_t)
    load_b = load(back_ref, back_t)
    load_order = load(order_ref, order_t)
    load_own = load(shard_ref, wbuf.at[lon])

    started = []

    def push(src, dst, ident, device):
        copy = pltpu.make_async_remote_copy(
            src_ref=src, dst_ref=dst, send_sem=send.at[ident], recv_sem=recv.at[ident],
            device_id=device, device_id_type=MESH,
        )
        copy.start()
        started.append(copy)

    def arrived(dst, ident, device):
        pltpu.make_async_remote_copy(
            src_ref=dst, dst_ref=dst, send_sem=send.at[ident], recv_sem=recv.at[ident],
            device_id=device, device_id_type=MESH,
        ).wait_recv()

    def slot(x, k, first=0, rows=64, c=core):
        return wbuf.at[x * 8 + k * 2 + c, pl.ds(first, rows)]

    def forward(ident, x, k, first, rows, device):
        push(slot(x, k, first, rows), slot(x, k, first, rows), ident, device)

    def got(ident, x, k, first, rows, device):
        arrived(slot(x, k, first, rows), ident, device)

    siblings = []

    def sibling(x, k, first, rows):
        ident = 25 + len(siblings)
        siblings.append((ident, x, k, first, rows))
        forward(ident, x, k, first, rows, dev_s)

    h1_ids, h2_ids = 7, 13
    sides = ((xm, dev_xm, dev_xp), (xp, dev_xp, dev_xm))

    def line(ident, k, first, rows):
        forward(ident, gx, k, first, rows, dev_xp)
        forward(ident + 1, gx, k, first, rows, dev_xm)

    def relay(ident, side, k, first, rows):
        x, source, target = sides[side]
        got(ident + side, x, k, first, rows, source)
        forward(ident + 2 + side, x, k, first + side * rows // 2, rows // 2, target)

    def far(ident, k, first, rows):
        for side, (_, source, _) in enumerate(sides):
            got(ident + 2 + side, xo, k, first + side * rows // 2, rows // 2, source)

    def gather(stage):
        if stage == 0:
            for ident, device in ((4, dev_o), (0, dev_xp), (1, dev_xm)):
                push(shard_ref, slot(gx, gk), ident, device)
            siblings.append((25, gx, gk, 0, 64))
            push(shard_ref, slot(gx, gk), 25, dev_s)
        elif stage == 1:
            push(shard_ref, slot(gx, gk), 6, dev_far)
        elif stage == 2:
            got(4, gx, ko, 0, 64, dev_o)
            forward(5, gx, ko, 0, 64, dev_i)
            line(h2_ids, ko, 32, 32)
            sibling(gx, ko, 0, 64)
            for side in range(2):
                x = sides[side][0]
                relay(0, side, gk, 0, 64)
                forward(h1_ids + 2 * side, x, gk, 0, 32, dev_o)
                sibling(x, gk, 0, 64)
        elif stage == 3:
            got(6, gx, kf, 0, 64, dev_far)
            line(h2_ids + 8, kf, 0, 64)
            sibling(gx, kf, 0, 64)
            far(0, gk, 0, 64)
            forward(h1_ids + 4, xo, gk, 0, 32, dev_o)
            sibling(xo, gk, 0, 64)
            for side in range(2):
                relay(h2_ids, side, ko, 32, 32)
            got(5, gx, ki, 0, 64, dev_i)
            line(h2_ids + 4, ki, 0, 64)
            sibling(gx, ki, 0, 64)
        elif stage == 4:
            for side in range(2):
                x = sides[side][0]
                got(h1_ids + 2 * side, x, ko, 0, 32, dev_o)
                sibling(x, ko, 0, 64)
            for side in range(2):
                relay(h2_ids + 8, side, kf, 0, 64)
                sibling(sides[side][0], kf, 0, 64)
        elif stage == 5:
            for side in range(2):
                relay(h2_ids + 4, side, ki, 0, 64)
                sibling(sides[side][0], ki, 0, 64)
            far(h2_ids, ko, 32, 32)
            got(h1_ids + 4, xo, ko, 0, 32, dev_o)
            sibling(xo, ko, 0, 64)
        else:
            far(h2_ids + 8, kf, 0, 64)
            sibling(xo, kf, 0, 64)
            far(h2_ids + 4, ki, 0, 64)
            sibling(xo, ki, 0, 64)

    gain = ngain_ref[...]
    load_x.wait()
    for at in range(0, TILE, 64):
        raw = xin[at // 4 : at // 4 + 16].astype(F32).reshape(64, WIDTH)
        xraw[at : at + 64] = raw.astype(BF16)
        mean = jnp.mean(raw, -1, keepdims=True)
        centered = raw - mean
        spread = jnp.mean(centered * centered, -1, keepdims=True)
        xn[at : at + 64] = (centered * lax.rsqrt(spread + 1e-05) * gain).astype(BF16)
    load_f.wait()
    for pair in range(2):
        fwd[pair] = dot(fwd_t[pair], xn[...]).astype(BF16)
        if pair == 0:
            pl.semaphore_wait(barrier, len(partners))
        for i, (at, rows) in enumerate(SENT):
            push(fwd.at[pair, pl.ds(at, rows)], rx.at[pair, pl.ds(at, rows)], 41 + 4 * pair + i, to[pair][i])

    gather(0)

    for pair in range(2):
        wrap = (lat == (nlat - 1 if pair == 0 else 0)).astype(jnp.int32)
        for w in range(2):
            codes = []
            for dim in range(2):
                at = lax.broadcasted_iota(jnp.int32, (WIN, WIN), dim)
                other = jnp.where(at < 72, 1, 0)
                level = ((at * 57) >> (11 - w)) & 1
                codes.append(other * wrap + 2 * level * pair)
            mask[pair, w] = jnp.where(codes[0] == codes[1], 1.0, 0.0)

    gather(1)
    load_q.wait()
    for pair in range(2):
        xquad[pair] = dot(quad_t[pair], xraw[...])

    gather(2)

    lane = lax.broadcasted_iota(jnp.int32, (1, 128), 1)
    low = jnp.where(lane < 64, 1.0, 0.0).astype(BF16)
    high = jnp.where(lane < 64, 0.0, 1.0).astype(BF16)

    def attend(pair, w, tokens):
        q = (dot(tokens, qkvw[:, :WIDTH]) * 0.125).astype(BF16)
        k = dot(tokens, qkvw[:, WIDTH : 2 * WIDTH]).astype(BF16)
        v = dot(tokens, qkvw[:, 2 * WIDTH :]).astype(BF16)
        same = mask[pair, w] > 0.5
        ones = jnp.ones((WIN, 128), BF16)
        for p in range(PAIRS):
            cols = slice(p * 128, (p + 1) * 128)
            both = jnp.concatenate([q[:, cols] * low, q[:, cols] * high], 0)
            scores = lax.dot_general(both, k[:, cols], (((1,), (1,)), ((), ())), preferred_element_type=F32)
            scores = jnp.where(same[None], scores.reshape(2, WIN, WIN), -1e30)
            top = jnp.max(scores, -1, keepdims=True)
            expo = jnp.exp(scores - top).astype(BF16).reshape(2 * WIN, WIN)
            result = dot(expo, jnp.concatenate([v[:, cols], ones], 1))
            result = result[:, :128] / result[:, 128:]
            att[pair, w, :, cols] = jnp.where(lane < 64, result[:WIN], result[WIN:]).astype(BF16)
        return dot(att[pair, w], projw[...]).astype(BF16)

    def send_back(pair, i):
        at, rows = SENT[i]
        push(bsend.at[pair, pl.ds(at, rows)], back.at[pair, pl.ds(at, rows)], 49 + 4 * pair + i, frm[pair][i])

    def await_piece(pair, i):
        at, rows = SENT[i]
        arrived(rx.at[pair, pl.ds(at, rows)], 41 + 4 * pair + i, frm[pair][i])

    load_qkv.wait()
    load_proj.wait()
    for pair in range(2):
        await_piece(pair, 0)
        s, own = rx.at[pair, pl.ds(0, 80)], fwd.at[pair, pl.ds(OWN, 80)]
        x = xw.at[pair, 0]
        x[0:64] = s[0:64]
        x[64:80] = s[64:80] + own[0:16]
        x[80:144] = own[16:80]
        branch = attend(pair, 0, x[...])
        bsend[pair, 0:80] = branch[0:80]
        send_back(pair, 0)
        back[pair, OWN : OWN + 80] = branch[64:144]

    for pair in range(2):
        for i in range(1, 4):
            await_piece(pair, i)
        s, l, d = (rx.at[pair, pl.ds(*SENT[i])] for i in range(1, 4))
        own = fwd.at[pair, pl.ds(OWN + 80, 48)]
        x = xw.at[pair, 1]
        x[0:32] = own[0:32]
        x[32:48] = own[32:48] + l[0:16]
        x[48:64] = l[16:32]
        x[64:80] = l[32:48] + s[0:16]
        x[80:96] = s[16:32]
        x[96:112] = s[32:48] + d[0:16]
        x[112:144] = d[16:48]
        branch = attend(pair, 1, x[...])
        bsend[pair, 80:128] = branch[64:112]
        bsend[pair, 128:176] = branch[32:80]
        bsend[pair, 176:224] = branch[96:144]
        for i in range(1, 4):
            send_back(pair, i)
        back[pair, OWN + 80 : PIECES] = branch[0:48]

    gather(3)
    gather(4)
    load_bq.wait()
    mgain = mgain_ref[...]
    for pair in range(2):
        for i, (at, rows) in enumerate(SENT):
            arrived(back.at[pair, pl.ds(at, rows)], 49 + 4 * pair + i, to[pair][i])
        if pair == 1:
            gather(5)
        quads = dot(backq_t[pair], back[pair]) + xquad[pair]
        quads = quads.astype(BF16).astype(F32).reshape(4, 72, WIDTH)
        mean = jnp.sum(jnp.sum(quads, 0), -1, keepdims=True) / (4 * WIDTH)
        centered = quads - mean
        spread = jnp.sum(jnp.sum(centered * centered, 0), -1, keepdims=True) / (4 * WIDTH)
        scale = lax.rsqrt(spread + 1e-05)
        for q in range(4):
            cols = slice(q * WIDTH, (q + 1) * WIDTH)
            mn[pair * 72 : (pair + 1) * 72, cols] = (centered[q] * scale * mgain[cols]).astype(BF16)

    load_b.wait()
    pieces = back[...].reshape(2 * PIECES, WIDTH)
    for at in range(0, TILE, 192):
        rows = dot(back_t[at : at + 192], pieces) + xraw[at : at + 192].astype(F32)
        out[at // 4 : at // 4 + 48] = rows.reshape(48, 4, WIDTH).astype(BF16)
    store_out = pltpu.make_async_copy(out, out_ref, local.at[9])
    store_out.start()

    gather(6)
    load_own.wait()
    load_order.wait()
    for ident, x, k, first, rows in siblings:
        arrived(slot(x, k, first, rows, 1 - core), ident, dev_s)

    def merge(n, carry):
        lanes = pl.ds(pl.multiple_of(n * 256, 256), 256)
        weight = wbuf[:, :, lanes].reshape(4 * WIDTH, 256)
        result = dot(mn[...], weight).astype(BF16)
        merged[:, :, lanes] = dot(order_t[...], result).reshape(36, 4, 256).astype(BF16)
        return carry

    lax.fori_loop(0, 4, merge, 0, unroll=True)
    store_merged = pltpu.make_async_copy(merged, coarse_ref, local.at[10])
    store_merged.start()

    for copy in started:
        copy.wait_send()
    store_out.wait()
    store_merged.wait()


def place(fine_ref, merged_ref, out_ref, coarse_ref, out, merged, came, left):
    parts = []
    for source, held, target in ((fine_ref, out, out_ref), (merged_ref, merged, coarse_ref)):
        rows = source.shape[0] // 4
        for i in range(4):
            at, part = pl.ds(i * rows, rows), len(parts)
            enter = pltpu.make_async_copy(source.at[at], held.at[at], came.at[part])
            enter.start()
            parts.append((enter, pltpu.make_async_copy(held.at[at], target.at[at], left.at[part])))
    for enter, leave in parts:
        enter.wait()
        leave.start()
    for _, leave in parts:
        leave.wait()


def local(fine_in, norm_gain, qkv_weight, proj_weight, merge_gain, merge_weight, *constants):
    anywhere = pl.BlockSpec(memory_space=pl.ANY)
    vmem = pl.BlockSpec(memory_space=pltpu.VMEM)
    scratch = [
        ((144, 4, WIDTH), BF16),
        ((TILE, WIDTH), BF16),
        ((TILE, WIDTH), BF16),
        ((2, PIECES, WIDTH), BF16),
        ((2, OWN, WIDTH), BF16),
        ((2, 2, WIN, WIDTH), BF16),
        ((2, 2, WIN, WIDTH), BF16),
        ((2, OWN, WIDTH), BF16),
        ((2, PIECES, WIDTH), BF16),
        ((2, 288, WIDTH), F32),
        ((2, 2, WIN, WIN), F32),
        ((144, 4 * WIDTH), BF16),
        ((36, 4, 2 * WIDTH), BF16),
        ((144, 4, WIDTH), BF16),
        ((32, 64, 2 * WIDTH), BF16),
        ((WIDTH, 3 * WIDTH), BF16),
        ((WIDTH, WIDTH), BF16),
        *((table.shape, BF16) for table in constants),
    ]
    tile = fine_in.transpose(1, 2, 0, 3).reshape(144, 4, WIDTH)
    out, coarse = pl.pallas_call(
        kernel,
        out_shape=(
            jax.ShapeDtypeStruct((144, 4, WIDTH), BF16),
            jax.ShapeDtypeStruct((36, 4, 2 * WIDTH), BF16),
        ),
        in_specs=[anywhere, vmem, anywhere, anywhere, vmem, anywhere] + [anywhere] * len(constants),
        out_specs=(anywhere, anywhere),
        scratch_shapes=[pltpu.VMEM(shape, dtype) for shape, dtype in scratch]
        + [pltpu.SemaphoreType.DMA((57,)), pltpu.SemaphoreType.DMA((57,)), pltpu.SemaphoreType.DMA((11,))],
        compiler_params=pltpu.CompilerParams(
            collective_id=0, has_side_effects=True, vmem_limit_bytes=56 * 1024 * 1024
        ),
        name="swin_block",
    )(tile, norm_gain, qkv_weight, proj_weight, merge_gain, merge_weight, *constants)
    fine_out, coarse = pl.pallas_call(
        place,
        out_shape=(jax.ShapeDtypeStruct(out.shape, BF16), jax.ShapeDtypeStruct(coarse.shape, BF16)),
        in_specs=[anywhere] * 2,
        out_specs=(anywhere, anywhere),
        scratch_shapes=[
            pltpu.VMEM(out.shape, BF16),
            pltpu.VMEM(coarse.shape, BF16),
            pltpu.SemaphoreType.DMA((8,)),
            pltpu.SemaphoreType.DMA((8,)),
        ],
        name="place",
    )(out, coarse)
    return (
        fine_out.reshape(12, 12, 4, WIDTH).transpose(2, 0, 1, 3),
        coarse.reshape(6, 6, 4, 2 * WIDTH).transpose(2, 0, 1, 3),
    )


def solution(mesh):
    grid = P(None, "lat", "lon", None)
    constants = tables()
    run = jax.shard_map(
        local,
        mesh=mesh,
        in_specs=(grid, P(), P(), P(), P(), P("lon", None), *(P() for _ in constants)),
        out_specs=(grid, grid),
        check_vma=False,
    )

    def whole(*arrays):
        return run(*arrays, *(jnp.asarray(table) for table in constants))

    return whole
```

profile of v0, /device:TPU:65, one launch (start us, length us, event | category | flops | bytes accessed | tf_op | source)
XLA Modules:
  0.0 48.7 jit_solution(3985591598638738720)
XLA Ops:
  0.6 46.0 %swin_block.1 = (bf16[144,4,512]{2,1,0:T(4,128)(2,1)}, bf16[36,4,1024]{2,1,0:T(4,128)(2,1)}) custom-call(bf16[144,4,512]{2,1,0:T(4,128)(2,1)} %bitcast.9, f32[512]{0:T(512)} %ngain_ref.1, bf16[512,1536]{1,0:T(8,128)(2,1)} %qkvw_ref.1, bf16[512,512]{1,0:T(8,128)(2,1)} %projw_ref.1, f32[2048]{0:T(1024)} %mgain_ref.1, bf16[64,1024]{1,0:T(8,128)(2,1)} %shard_ref.1, ...), custom_call_target="tpu_custom_call" | custom-call | tf_op jit(solution)/shard_map/swin_block/pallas_call | solution.py:405
  46.6 2.0 %place.1 = (bf16[144,4,512]{2,1,0:T(4,128)(2,1)}, bf16[36,4,1024]{2,1,0:T(4,128)(2,1)}) custom-call(bf16[144,4,512]{2,1,0:T(4,128)(2,1)} %get-tuple-element.6.fine_ref, bf16[36,4,1024]{2,1,0:T(4,128)(2,1)} %get-tuple-element.7.merged_ref), custom_call_target="tpu_custom_call" | custom-call | tf_op jit(solution)/shard_map/place/pallas_call | solution.py:420
where the time goes:
time: 48.8 us; the launch traced here: 48.7 us
  Pallas kernels  48 us (98%)
  between operations  0.64 us (1%)
    pallas_call x1, Pallas kernels, local(): pl.pallas_call(kernel, out_shape=(jax.ShapeDtypeStruct((144, 4, WIDTH), B...  46 us
    pallas_call x1, Pallas kernels, local(): pl.pallas_call(place, out_shape=(jax.ShapeDtypeStruct(out.shape, BF16), j...  2.02 us

commit v1 on v0

--- a/solution.py
+++ b/solution.py
@@ -345,21 +345,20 @@
     for ident, x, k, first, rows in siblings:
         arrived(slot(x, k, first, rows, 1 - core), ident, dev_s)
 
-    def merge(n, carry):
-        lanes = pl.ds(pl.multiple_of(n * 256, 256), 256)
+    stores = [store_out]
+    for n in range(4):
+        lanes = pl.ds(n * 256, 256)
         weight = wbuf[:, :, lanes].reshape(4 * WIDTH, 256)
         result = dot(mn[...], weight).astype(BF16)
         merged[:, :, lanes] = dot(order_t[...], result).reshape(36, 4, 256).astype(BF16)
-        return carry
-
-    lax.fori_loop(0, 4, merge, 0, unroll=True)
-    store_merged = pltpu.make_async_copy(merged, coarse_ref, local.at[10])
-    store_merged.start()
+        store = pltpu.make_async_copy(merged.at[:, :, lanes], coarse_ref.at[:, :, lanes], local.at[10 + n])
+        store.start()
+        stores.append(store)
 
     for copy in started:
         copy.wait_send()
-    store_out.wait()
-    store_merged.wait()
+    for store in stores:
+        store.wait()
 
 
 def place(fine_ref, merged_ref, out_ref, coarse_ref, out, merged, came, left):
@@ -411,7 +410,7 @@
         in_specs=[anywhere, vmem, anywhere, anywhere, vmem, anywhere] + [anywhere] * len(constants),
         out_specs=(anywhere, anywhere),
         scratch_shapes=[pltpu.VMEM(shape, dtype) for shape, dtype in scratch]
-        + [pltpu.SemaphoreType.DMA((57,)), pltpu.SemaphoreType.DMA((57,)), pltpu.SemaphoreType.DMA((11,))],
+        + [pltpu.SemaphoreType.DMA((57,)), pltpu.SemaphoreType.DMA((57,)), pltpu.SemaphoreType.DMA((14,))],
         compiler_params=pltpu.CompilerParams(
             collective_id=0, has_side_effects=True, vmem_limit_bytes=56 * 1024 * 1024
         ),

time: 48.8 us -> 48.8 us (level)
  no operation moved by 1% of the time
where the time goes in v1:
time: 48.8 us; the launch traced here: 48.6 us
  Pallas kernels  48 us (98%)
  between operations  0.64 us (1%)
    pallas_call x1, Pallas kernels, local(): pl.pallas_call(kernel, out_shape=(jax.ShapeDtypeStruct((144, 4, WIDTH), B...  45.9 us
    pallas_call x1, Pallas kernels, local(): pl.pallas_call(place, out_shape=(jax.ShapeDtypeStruct(out.shape, BF16), j...  2.02 us

profile of v1, /device:TPU:65, one launch (start us, length us, event | category | flops | bytes accessed | tf_op | source)
XLA Modules:
  0.0 48.6 jit_solution(17609557909328305419)
XLA Ops:
  0.6 45.9 %swin_block.1 = (bf16[144,4,512]{2,1,0:T(4,128)(2,1)}, bf16[36,4,1024]{2,1,0:T(4,128)(2,1)}) custom-call(bf16[144,4,512]{2,1,0:T(4,128)(2,1)} %bitcast.9, f32[512]{0:T(512)} %ngain_ref.1, bf16[512,1536]{1,0:T(8,128)(2,1)} %qkvw_ref.1, bf16[512,512]{1,0:T(8,128)(2,1)} %projw_ref.1, f32[2048]{0:T(1024)} %mgain_ref.1, bf16[64,1024]{1,0:T(8,128)(2,1)} %shard_ref.1, ...), custom_call_target="tpu_custom_call" | custom-call | tf_op jit(solution)/shard_map/swin_block/pallas_call | solution.py:404
  46.6 2.0 %place.1 = (bf16[144,4,512]{2,1,0:T(4,128)(2,1)}, bf16[36,4,1024]{2,1,0:T(4,128)(2,1)}) custom-call(bf16[144,4,512]{2,1,0:T(4,128)(2,1)} %get-tuple-element.6.fine_ref, bf16[36,4,1024]{2,1,0:T(4,128)(2,1)} %get-tuple-element.7.merged_ref), custom_call_target="tpu_custom_call" | custom-call | tf_op jit(solution)/shard_map/place/pallas_call | solution.py:419
